TPU v7x, 32 devices: a whole 2x2x4 slice. The times are simulated.
32 devices in a mesh: expert: 4 (over x, core), context: 2 (over y), dp: 4 (over z).
Axes of the slice: x: 2, y: 2, z: 4, core: 2. Of those that a mesh axis runs over, the one named last changes fastest.
Arguments:
- tokens: bfloat16 [16, 512, 1024], P(('expert', 'dp'), 'context'), may hold values from -6 to 6
- span_order: int32 [4], replicated, may hold values from 0 to 3, each once
- routes: int32 [16, 512, 8], P(('expert', 'dp'), 'context'), may hold values from 0 to 15, all different within a row; in each aligned block of 256 rows (0 to 255, 256 to 511, ..., all dimensions but the last counted through in order) at most 160 rows name the same one
- norm_attn: bfloat16 [1024], replicated, may hold values from 0.5 to 1.5
- w_query: bfloat16 [1024, 1024], replicated, may hold values from -0.1875 to 0.1875
- w_key: bfloat16 [1024, 512], replicated, may hold values from -0.1875 to 0.1875
- w_value: bfloat16 [1024, 512], replicated, may hold values from -0.1875 to 0.1875
- w_out: bfloat16 [1024, 1024], replicated, may hold values from -1.5 to 1.5
- norm_moe: bfloat16 [1024], replicated, may hold values from 0.5 to 1.5
- w_router: bfloat16 [1024, 16], replicated, may hold values from -0.09375 to 0.09375
- w_gate: bfloat16 [16, 1024, 512], P('expert'), may hold values from -0.1875 to 0.1875
- w_up: bfloat16 [16, 1024, 512], P('expert'), may hold values from -0.1875 to 0.1875
- w_down: bfloat16 [16, 512, 1024], P('expert'), may hold values from -1 to 1
- cotangent: bfloat16 [16, 512, 1024], P(('expert', 'dp'), 'context'), may hold values from -6 to 6
Outputs:
- outputs: bfloat16 [16, 512, 1024], P(('expert', 'dp'), 'context')
- grad_tokens: bfloat16 [16, 512, 1024], P(('expert', 'dp'), 'context')
- grad_norm_attn: float32 [1024], replicated
- grad_query: float32 [1024, 1024], replicated
- grad_key: float32 [1024, 512], replicated
- grad_value: float32 [1024, 512], replicated
- grad_out: float32 [1024, 1024], replicated
- grad_norm_moe: float32 [1024], replicated
- grad_router: float32 [1024, 16], replicated
- grad_gate: float32 [16, 1024, 512], P('expert')
- grad_up: float32 [16, 1024, 512], P('expert')
- grad_down: float32 [16, 512, 1024], P('expert')
Inputs may be any that keep to these rules, and one draw needn't show every extreme that they name: span_order is a permutation; stored block j of every sequence holds the tokens at positions span_order[j] * 128 to span_order[j] * 128 + 127. `routes`: each token names 8 different experts. Within the rows of one device (aligned blocks of 256 rows, in order), no expert is named by more than 160 rows, a bound that some block reaches.
All inputs are finite; a program needn't handle non-finite values.
Results may differ from a plain program's by a relative error of at most 0.017.
Values may be sent and summed in bfloat16 or wider, within the bound.
A program may use at most 192 MiB of HBM per device.

v0:
```python
import math
import jax
import jax.numpy as jnp
from jax import lax
from jax.sharding import PartitionSpec as P

D = 1024
H = 16
KV = 8
HD = 64
TOP = 8
EXPERTS = 16
CAP = 160
SPAN = 128
EPSILON = 1e-06
ROPE_BASE = 10000.0
MASKED = -1e30


def rope_tables(positions):
    half_dim = HD // 2
    frequency = ROPE_BASE ** (-(jnp.arange(half_dim, dtype=jnp.float32) * 2.0) / HD)
    angles = positions.astype(jnp.float32)[:, None] * frequency[None, :]
    return (jnp.cos(angles), jnp.sin(angles))


def rotate(tensor, cos_table, sin_table):
    half_dim = tensor.shape[-1] // 2
    front_half = tensor[..., :half_dim]
    back_half = tensor[..., half_dim:]
    cos_wide = cos_table[:, None, :]
    sin_wide = sin_table[:, None, :]
    return jnp.concatenate(
        [
            front_half * cos_wide - back_half * sin_wide,
            back_half * cos_wide + front_half * sin_wide,
        ],
        axis=-1,
    )


def rotate_back(tensor, cos_table, sin_table):
    half_dim = tensor.shape[-1] // 2
    front_grad = tensor[..., :half_dim]
    back_grad = tensor[..., half_dim:]
    cos_wide = cos_table[:, None, :]
    sin_wide = sin_table[:, None, :]
    return jnp.concatenate(
        [
            front_grad * cos_wide + back_grad * sin_wide,
            back_grad * cos_wide - front_grad * sin_wide,
        ],
        axis=-1,
    )


def slot_tables(route_rows):
    flat_ids = route_rows.reshape(-1)
    assignments = flat_ids.shape[0]
    one_hot = (flat_ids[:, None] == jnp.arange(EXPERTS, dtype=jnp.int32)[None, :]).astype(jnp.int32)
    earlier = jnp.cumsum(one_hot, axis=0, dtype=jnp.int32) - one_hot
    within = jnp.sum(earlier * one_hot, axis=1, dtype=jnp.int32)
    target = flat_ids * CAP + within
    source = (
        jnp.full((EXPERTS * CAP,), assignments, jnp.int32)
        .at[target]
        .set(jnp.arange(assignments, dtype=jnp.int32))
    )
    filled = source < assignments
    return (target, jnp.minimum(source, assignments - 1), filled)


def positions_of(row_index, span_order):
    block_ids = row_index // SPAN
    picked = jnp.where(
        block_ids[:, None] == jnp.arange(span_order.shape[0], dtype=jnp.int32)[None, :],
        span_order[None, :],
        0,
    )
    return jnp.sum(picked, axis=1, dtype=jnp.int32) * SPAN + row_index % SPAN


def norm_back(grad_normed, normed, inv_root):
    return inv_root * (
        grad_normed - normed * jnp.mean(grad_normed * normed, axis=-1, keepdims=True)
    )


def body(
    tokens,
    span_order,
    routes,
    norm_attn,
    w_query,
    w_key,
    w_value,
    w_out,
    norm_moe,
    w_router,
    w_gate,
    w_up,
    w_down,
    cotangent,
):
    tok_rows = tokens.shape[1]
    seq_rows = tok_rows * lax.axis_size("context")
    groups = H // KV
    score_scale = 1.0 / math.sqrt(HD)
    local_experts = w_gate.shape[0]
    expert_groups = lax.axis_size("expert")
    local_index = lax.axis_index("context") * tok_rows + jnp.arange(tok_rows, dtype=jnp.int32)
    pos_query = positions_of(local_index, span_order)
    pos_keys = positions_of(jnp.arange(seq_rows, dtype=jnp.int32), span_order)
    cos_table, sin_table = rope_tables(pos_query)
    allowed = pos_keys[None, :] <= pos_query[:, None]
    inputs = tokens[0].astype(jnp.float32)
    inv_one = lax.rsqrt(jnp.mean(inputs * inputs, axis=-1, keepdims=True) + EPSILON)
    normed_one = inputs * inv_one
    gain_one = norm_attn.astype(jnp.float32)
    h_one = (normed_one * gain_one).astype(jnp.bfloat16)
    query_pre = jnp.dot(h_one, w_query, preferred_element_type=jnp.float32).reshape(tok_rows, H, HD)
    queries = (
        rotate(query_pre, cos_table, sin_table)
        .astype(jnp.bfloat16)
        .reshape(tok_rows, KV, groups, HD)
    )
    key_pre = jnp.dot(h_one, w_key, preferred_element_type=jnp.float32).reshape(tok_rows, KV, HD)
    keys_local = (
        rotate(key_pre, cos_table, sin_table).astype(jnp.bfloat16).reshape(tok_rows, KV * HD)
    )
    values_local = jnp.dot(h_one, w_value, preferred_element_type=jnp.float32).astype(jnp.bfloat16)
    keys_all, values_all = (
        lax.all_gather(keys_local, "context", axis=0, tiled=True),
        lax.all_gather(values_local, "context", axis=0, tiled=True),
    )
    scores = (
        jnp.einsum(
            "qkgd,skd->kgqs",
            queries,
            keys_all.reshape(seq_rows, KV, HD),
            preferred_element_type=jnp.float32,
        )
        * score_scale
    )
    masked = jnp.where(allowed, scores, MASKED)
    top_score = jnp.max(masked, axis=-1, keepdims=True)
    exp_scores = jnp.exp(masked - top_score)
    total_exp = jnp.sum(exp_scores, axis=-1, keepdims=True)
    attn_probs = exp_scores / total_exp
    log_total = top_score + jnp.log(total_exp)
    mixed_heads = jnp.einsum(
        "kgqs,skd->qkgd",
        attn_probs.astype(jnp.bfloat16),
        values_all.reshape(seq_rows, KV, HD),
        preferred_element_type=jnp.float32,
    )
    mixed_heads = mixed_heads.reshape(tok_rows, H * HD).astype(jnp.bfloat16)
    y_one = inputs + jnp.dot(mixed_heads, w_out, preferred_element_type=jnp.float32)
    inv_two = lax.rsqrt(jnp.mean(y_one * y_one, axis=-1, keepdims=True) + EPSILON)
    normed_two = y_one * inv_two
    gain_two = norm_moe.astype(jnp.float32)
    h_two = (normed_two * gain_two).astype(jnp.bfloat16)
    logits = jnp.dot(h_two, w_router, preferred_element_type=jnp.float32)
    route_rows = routes[0]
    chosen_mask = route_rows[:, :, None] == jnp.arange(EXPERTS, dtype=jnp.int32)[None, None, :]
    chosen = jnp.sum(jnp.where(chosen_mask, logits[:, None, :], 0.0), axis=-1)
    chosen_exp = jnp.exp(chosen - jnp.max(chosen, axis=-1, keepdims=True))
    route_weights = chosen_exp / jnp.sum(chosen_exp, axis=-1, keepdims=True)
    target, source, filled = slot_tables(route_rows)
    sent_rows = jnp.where(
        filled[:, None], jnp.take(h_two, source // TOP, axis=0), jnp.zeros((), jnp.bfloat16)
    )
    sent_rows = sent_rows.reshape(expert_groups, local_experts, CAP, D)
    received = lax.all_to_all(sent_rows, "expert", split_axis=0, concat_axis=0, tiled=True)
    gate_pre = jnp.einsum("necd,edf->necf", received, w_gate, preferred_element_type=jnp.float32)
    upward = jnp.einsum("necd,edf->necf", received, w_up, preferred_element_type=jnp.float32)
    sigmoid_gate = jax.nn.sigmoid(gate_pre)
    silu_gate = gate_pre * sigmoid_gate
    hidden = (silu_gate * upward).astype(jnp.bfloat16)
    produced = jnp.einsum(
        "necf,efd->necd", hidden, w_down, preferred_element_type=jnp.float32
    ).astype(jnp.bfloat16)
    returned = lax.all_to_all(produced, "expert", split_axis=0, concat_axis=0, tiled=True).reshape(
        EXPERTS * CAP, D
    )
    gathered = jnp.take(returned, target, axis=0).reshape(tok_rows, TOP, D).astype(jnp.float32)
    y_two = jnp.sum(route_weights[:, :, None] * gathered, axis=1)
    outputs = (y_one + y_two).astype(jnp.bfloat16)[None]
    grad_final = cotangent[0].astype(jnp.float32)
    grad_gathered = route_weights[:, :, None] * grad_final[:, None, :]
    grad_weights = jnp.sum(grad_final[:, None, :] * gathered, axis=-1)
    grad_slots = jnp.where(
        filled[:, None], jnp.take(grad_gathered.reshape(-1, D), source, axis=0), 0.0
    )
    grad_slots = grad_slots.astype(jnp.bfloat16).reshape(expert_groups, local_experts, CAP, D)
    grad_received = lax.all_to_all(grad_slots, "expert", split_axis=0, concat_axis=0, tiled=True)
    grad_hidden = jnp.einsum(
        "necd,efd->necf", grad_received, w_down, preferred_element_type=jnp.float32
    )
    grad_down_w = jnp.einsum(
        "necf,necd->efd", hidden, grad_received, preferred_element_type=jnp.float32
    )
    grad_gate_pre = (
        grad_hidden * upward * sigmoid_gate * (1.0 + gate_pre * (1.0 - sigmoid_gate))
    ).astype(jnp.bfloat16)
    grad_up_pre = (grad_hidden * silu_gate).astype(jnp.bfloat16)
    grad_gate_w = jnp.einsum(
        "necd,necf->edf", received, grad_gate_pre, preferred_element_type=jnp.float32
    )
    grad_up_w = jnp.einsum(
        "necd,necf->edf", received, grad_up_pre, preferred_element_type=jnp.float32
    )
    grad_sent = jnp.einsum(
        "necf,edf->necd", grad_gate_pre, w_gate, preferred_element_type=jnp.float32
    )
    grad_sent = (
        grad_sent
        + jnp.einsum("necf,edf->necd", grad_up_pre, w_up, preferred_element_type=jnp.float32)
    ).astype(jnp.bfloat16)
    grad_back = lax.all_to_all(
        grad_sent, "expert", split_axis=0, concat_axis=0, tiled=True
    ).reshape(EXPERTS * CAP, D)
    grad_h_two = jnp.sum(
        jnp.take(grad_back, target, axis=0).reshape(tok_rows, TOP, D).astype(jnp.float32), axis=1
    )
    grad_chosen = route_weights * (
        grad_weights - jnp.sum(route_weights * grad_weights, axis=-1, keepdims=True)
    )
    grad_logits = jnp.sum(jnp.where(chosen_mask, grad_chosen[:, :, None], 0.0), axis=1).astype(
        jnp.bfloat16
    )
    grad_router_w = jnp.einsum("td,te->de", h_two, grad_logits, preferred_element_type=jnp.float32)
    grad_h_two = grad_h_two + jnp.einsum(
        "te,de->td", grad_logits, w_router, preferred_element_type=jnp.float32
    )
    grad_gain_two = jnp.sum(grad_h_two * normed_two, axis=0)
    grad_y_one = grad_final + norm_back(grad_h_two * gain_two, normed_two, inv_two)
    grad_attn = grad_y_one.astype(jnp.bfloat16)
    grad_out_w = jnp.einsum("tm,td->md", mixed_heads, grad_attn, preferred_element_type=jnp.float32)
    grad_mixed = jnp.einsum(
        "td,md->tm", grad_attn, w_out, preferred_element_type=jnp.float32
    ).astype(jnp.bfloat16)
    grad_mixed = grad_mixed.reshape(tok_rows, KV, groups, HD)
    keys_back, values_back = (
        lax.all_gather(keys_local, "context", axis=0, tiled=True),
        lax.all_gather(values_local, "context", axis=0, tiled=True),
    )
    key_heads = keys_back.reshape(seq_rows, KV, HD)
    scores_back = (
        jnp.einsum("qkgd,skd->kgqs", queries, key_heads, preferred_element_type=jnp.float32)
        * score_scale
    )
    probs_back = jnp.where(allowed, jnp.exp(scores_back - log_total), 0.0)
    grad_probs = jnp.einsum(
        "qkgd,skd->kgqs",
        grad_mixed,
        values_back.reshape(seq_rows, KV, HD),
        preferred_element_type=jnp.float32,
    )
    grad_values = jnp.einsum(
        "kgqs,qkgd->skd",
        probs_back.astype(jnp.bfloat16),
        grad_mixed,
        preferred_element_type=jnp.float32,
    )
    row_dots = jnp.sum(probs_back * grad_probs, axis=-1, keepdims=True)
    grad_scores = (probs_back * (grad_probs - row_dots)).astype(jnp.bfloat16)
    grad_queries = (
        jnp.einsum("kgqs,skd->qkgd", grad_scores, key_heads, preferred_element_type=jnp.float32)
        * score_scale
    )
    grad_keys = (
        jnp.einsum("kgqs,qkgd->skd", grad_scores, queries, preferred_element_type=jnp.float32)
        * score_scale
    )
    grad_keys_mine, grad_values_mine = (
        lax.psum_scatter(
            grad_keys.reshape(seq_rows, KV * HD), "context", scatter_dimension=0, tiled=True
        ),
        lax.psum_scatter(
            grad_values.reshape(seq_rows, KV * HD), "context", scatter_dimension=0, tiled=True
        ),
    )
    grad_q_pre = (
        rotate_back(grad_queries.reshape(tok_rows, H, HD), cos_table, sin_table)
        .reshape(tok_rows, H * HD)
        .astype(jnp.bfloat16)
    )
    grad_k_pre = (
        rotate_back(grad_keys_mine.reshape(tok_rows, KV, HD), cos_table, sin_table)
        .reshape(tok_rows, KV * HD)
        .astype(jnp.bfloat16)
    )
    grad_v_pre = grad_values_mine.astype(jnp.bfloat16)
    grad_query_w = jnp.einsum("td,tm->dm", h_one, grad_q_pre, preferred_element_type=jnp.float32)
    grad_key_w = jnp.einsum("td,tm->dm", h_one, grad_k_pre, preferred_element_type=jnp.float32)
    grad_value_w = jnp.einsum("td,tm->dm", h_one, grad_v_pre, preferred_element_type=jnp.float32)
    grad_h_one = jnp.einsum("tm,dm->td", grad_q_pre, w_query, preferred_element_type=jnp.float32)
    grad_h_one = grad_h_one + jnp.einsum(
        "tm,dm->td", grad_k_pre, w_key, preferred_element_type=jnp.float32
    )
    grad_h_one = grad_h_one + jnp.einsum(
        "tm,dm->td", grad_v_pre, w_value, preferred_element_type=jnp.float32
    )
    grad_gain_one = jnp.sum(grad_h_one * normed_one, axis=0)
    grad_inputs = grad_y_one + norm_back(grad_h_one * gain_one, normed_one, inv_one)
    grad_tokens = grad_inputs.astype(jnp.bfloat16)[None]
    total_gate, total_up, total_down = (
        lax.psum(grad_gate_w.astype(jnp.bfloat16), ("context", "dp")).astype(jnp.float32),
        lax.psum(grad_up_w.astype(jnp.bfloat16), ("context", "dp")).astype(jnp.float32),
        lax.psum(grad_down_w.astype(jnp.bfloat16), ("context", "dp")).astype(jnp.float32),
    )
    total_g1, total_q, total_k, total_v, total_o, total_g2, total_r = lax.psum(
        (
            grad_gain_one,
            grad_query_w,
            grad_key_w,
            grad_value_w,
            grad_out_w,
            grad_gain_two,
            grad_router_w,
        ),
        ("expert", "context", "dp"),
    )
    return (
        outputs,
        grad_tokens,
        total_g1,
        total_q,
        total_k,
        total_v,
        total_o,
        total_g2,
        total_r,
        total_gate,
        total_up,
        total_down,
    )


def solution(mesh):
    in_specs = (
        P(("expert", "dp"), "context", None),
        P(),
        P(("expert", "dp"), "context", None),
        P(),
        P(),
        P(),
        P(),
        P(),
        P(),
        P(),
        P("expert", None, None),
        P("expert", None, None),
        P("expert", None, None),
        P(("expert", "dp"), "context", None),
    )
    out_specs = (
        P(("expert", "dp"), "context", None),
        P(("expert", "dp"), "context", None),
        P(),
        P(),
        P(),
        P(),
        P(),
        P(),
        P(),
        P("expert", None, None),
        P("expert", None, None),
        P("expert", None, None),
    )
    return jax.shard_map(body, mesh=mesh, in_specs=in_specs, out_specs=out_specs, check_vma=False)
```

profile of v0, /device:TPU:0, one launch (start us, length us, event | category | flops | bytes accessed | tf_op | source)
XLA Modules:
  0.0 1157.8 jit_solution(6361689802056740667)
XLA Ops:
  13.8 9.9 all_gather.8
  30.6 8.2 all_gather.9
  38.8 4.1 copy.81
  42.9 2.4 fusion.70
  53.3 4.5 reduce-window.6
  58.7 8.1 scatter_custom_fusion
  68.4 8.8 gather_fusion
  77.2 3.7 select_select_fusion
  80.9 62.5 %all_to_all.20 = bf16[4,4,160,1024]{3,2,1,0:T(8,128)(2,1)S(1)} all-to-all(bf16[4,4,160,1024]{3,2,1,0:T(8,128)(2,1)S(1)} %select_select_fusion), channel_id=1, replica_groups=mesh['expert'=4,'context'=2,'dp'=4] {'expert'}, dimensions={0} | all-to-all | bytes 10485760 | tf_op jit(solution)/shard_map/all_to_all | solution.py:174
  143.4 2.9 fusion.26
  147.4 5.4 fusion.15
  153.1 4.9 convert_bitcast_fusion.1
  157.9 3.3 copy.89
  161.2 5.2 all-to-all-start.1
  168.0 57.9 %all-to-all-done.1 = bf16[4,4,160,1024]{3,2,1,0:T(8,128)(2,1)} async-done(((bf16[4,4,160,1024]{3,2,1,0:T(8,128)(2,1)}), bf16[4,4,160,1024]{3,2,1,0:T(8,128)(2,1)}, u32[]{:S(2)}, u32[]{:S(2)}) %all-to-all-start.1) | async-done | bytes 5242912 | tf_op jit(solution)/shard_map/all_to_all | solution.py:183
  225.9 14.1 %gather_fusion.2 = bf16[2048,1024]{1,0:T(8,128)(2,1)} fusion(bf16[2560,1024]{1,0:T(8,128)(2,1)} %bitcast.33, s32[2048]{0:T(1024)S(1)} %broadcast_clamp_fusion), kind=kCustom, calls=%fused_computation.clone | custom fusion | bytes 8396800 | tf_op jit(solution)/shard_map/jit(_take)/gather | solution.py:186
  240.0 3.3 fusion.2
  243.7 3.4 bitcast_multiply_fusion.1
  247.1 14.8 %gather_fusion.1 = bf16[2560,1024]{1,0:T(8,128)(2,1)} fusion(bf16[2048,1024]{1,0:T(8,128)(2,1)} %bitcast_multiply_fusion.1, s32[3072]{0:T(1024)S(1)} %pad_clamp_fusion), kind=kCustom, calls=%fused_computation.3 | custom fusion | bytes 10496000 | tf_op jit(solution)/shard_map/jit(_take)/gather | solution.py:193
  261.9 4.0 select_convert_fusion
  265.9 63.3 %all_to_all.21 = bf16[4,4,160,1024]{3,2,1,0:T(8,128)(2,1)} all-to-all(bf16[4,4,160,1024]{3,2,1,0:T(8,128)(2,1)S(1)} %select_convert_fusion), channel_id=1, replica_groups=mesh['expert'=4,'context'=2,'dp'=4] {'expert'}, dimensions={0} | all-to-all | bytes 10485760 | tf_op jit(solution)/shard_map/all_to_all | solution.py:196
  329.2 12.7 %fusion.13 = (bf16[4,4,160,512]{3,2,0,1:T(8,128)(2,1)}, bf16[4,4,160,512]{3,2,0,1:T(8,128)(2,1)S(1)}) fusion(f32[4,4,160,512]{3,2,1,0:T(8,128)} %get-tuple-element.56, f32[4,4,160,512]{3,2,1,0:T(8,128)} %copy-done.45, bf16[4,512,1024]{2,1,0:T(8,128)(2,1)} %param.28, bf16[4,4,160,1024]{3,2,1,0:T(8,128)(2,1)} %all_to_all.21), kind=kOutput, calls=%fused_computation.35 | convolution fusion | flops 2701393920 | bytes 25165824 | tf_op jit(solution)/shard_map/necd,efd->necf/dot_general | solution.py:197
  342.0 8.6 fusion.29
  350.6 8.9 fusion.10
  359.5 3.0 copy.92
  362.5 5.1 all-to-all-start.3
  367.9 59.2 %all-to-all-done.3 = bf16[4,4,160,1024]{3,2,1,0:T(8,128)(2,1)} async-done(((bf16[4,4,160,1024]{3,2,1,0:T(8,128)(2,1)}), bf16[4,4,160,1024]{3,2,1,0:T(8,128)(2,1)}, u32[]{:S(2)}, u32[]{:S(2)}) %all-to-all-start.3) | async-done | bytes 5242912 | tf_op jit(solution)/shard_map/all_to_all | solution.py:220
  427.1 14.1 %gather_fusion.3 = bf16[2048,1024]{1,0:T(8,128)(2,1)} fusion(bf16[2560,1024]{1,0:T(8,128)(2,1)} %bitcast.45, s32[2048]{0:T(1024)S(1)} %broadcast_clamp_fusion), kind=kCustom, calls=%fused_computation.1.clone | custom fusion | bytes 8396800 | tf_op jit(solution)/shard_map/jit(_take)/gather | solution.py:224
  441.2 8.1 convert_reduce_fusion
  455.5 5.3 fusion.3
  461.6 2.4 fusion.5
  468.5 6.2 fusion.38
  475.0 8.9 bitcast_convert_fusion.2
  483.9 8.4 bitcast_convert_fusion.1
  492.4 5.1 bitcast_convert_fusion
  498.6 3.0 convolution_multiply_fusion
  502.0 3.1 fusion.76
  505.0 2.7 fusion.79
  512.6 2.9 fusion.82
  515.6 2.5 fusion.124
  521.6 42.8 %all-reduce = (f32[1024]{0:T(1024)}, f32[1024]{0:T(1024)}) all-reduce(f32[1024]{0:T(1024)S(1)} %get-tuple-element.15, f32[1024]{0:T(1024)S(1)} %get-tuple-element.13), channel_id=1, replica_groups=mesh['expert'=4,'context'=2,'dp'=4] {'expert','context','dp'}, use_global_device_ids=true, to_apply=%region_24.26 | all-reduce | flops 2048 | bytes 16384 | tf_op jit(solution)/shard_map/psum | solution.py:313
  564.3 2.6 fusion.69
  567.0 328.1 %all-reduce.8.cloned.1.call-done = (bf16[4,1024,512]{2,1,0:T(8,128)(2,1)}, bf16[4,1024,512]{2,1,0:T(8,128)(2,1)}, bf16[4,512,1024]{2,1,0:T(8,128)(2,1)}) async-done(((bf16[4,1024,512]{2,1,0:T(8,128)(2,1)}, bf16[4,1024,512]{2,1,0:T(8,128)(2,1)}, bf16[4,512,1024]{2,1,0:T(8,128)(2,1)}), (bf16[4,1024,512]{2,1,0:T(8,128)(2,1)}, bf16[4,1024,512]{2,1,0:T(8,128)(2,1)}, ...) | async-done | bytes 12582928 | tf_op jit(solution)/shard_map/psum | solution.py:309
  895.1 6.9 convert_element_type.232
  902.0 4.6 convert_element_type.234
  906.6 4.5 convert_element_type.236
  911.0 227.6 %all-reduce.6.cloned.1.call-done = (f32[1024,1024]{1,0:T(8,128)}, f32[1024,512]{1,0:T(8,128)}, f32[1024,512]{1,0:T(8,128)}, f32[1024,1024]{1,0:T(8,128)}, f32[1024,16]{0,1:T(8,128)}) async-done(((f32[1024,1024]{1,0:T(8,128)}, f32[1024,512]{1,0:T(8,128)}, f32[1024,512]{1,0:T(8,128)}, f32[1024,1024]{1,0:T(8,128)}, f32[1024,16]{0,1:T(8,128)}), (f32[1024,1024]{1,0:T(8,128)}, f32[1024,512]{1,0:T(8,128)}, ...) | async-done | bytes 12648464 | tf_op jit(solution)/shard_map/psum | solution.py:313
  1138.7 4.9 copy.142
  (194 shorter events, 54.3 us)
Async XLA Ops:
  8.0 43.3 %copy-start = (bf16[1024,1024]{1,0:T(8,128)(2,1)S(1)}, bf16[1024,1024]{1,0:T(8,128)(2,1)}, u32[]{:S(2)}) copy-start(bf16[1024,1024]{1,0:T(8,128)(2,1)} %param.23) | copy-start | bytes 6291460
  8.0 20.5 %copy-start.3 = (bf16[1,256,1024]{2,1,0:T(8,128)(2,1)S(1)}, bf16[1,256,1024]{2,1,0:T(8,128)(2,1)}, u32[]{:S(2)}) copy-start(bf16[1,256,1024]{2,1,0:T(8,128)(2,1)} %param.16) | copy-start | bytes 1572868
  10.7 32.2 %copy-start.36 = (f32[1024]{0:T(1024)}, f32[1024]{0:T(1024)S(1)}, u32[]{:S(2)}) copy-start(f32[1024]{0:T(1024)S(1)} %convert_element_type.188) | copy-start | bytes 12292
  11.9 31.0 %copy-start.41 = (f32[256]{0:T(256)}, f32[256]{0:T(256)S(1)}, u32[]{:S(2)}) copy-start(f32[256]{0:T(256)S(1)} %add_rsqrt_fusion.1) | copy-start | bytes 3076
  30.5 15.0 %copy-start.32 = (f32[256,32]{0,1:T(8,128)}, f32[256,32]{0,1:T(8,128)S(1)}, u32[]{:S(2)}) copy-start(f32[256,32]{0,1:T(8,128)S(1)} %get-tuple-element.49) | copy-start | bytes 98308
  30.5 15.0 %copy-start.34 = (f32[256,32]{0,1:T(8,128)}, f32[256,32]{0,1:T(8,128)S(1)}, u32[]{:S(2)}) copy-start(f32[256,32]{0,1:T(8,128)S(1)} %get-tuple-element.50) | copy-start | bytes 98308
  38.8 8.3 copy-start.8
  47.1 4.2 copy-start.1
  48.9 4.2 copy-start.43
  51.3 25.9 %copy-start.28 = (bf16[8,64,2,256]{3,1,2,0:T(8,128)(2,1)}, bf16[8,64,2,256]{3,1,2,0:T(8,128)(2,1)S(1)}, u32[]{:S(2)}) copy-start(bf16[8,64,2,256]{3,1,2,0:T(8,128)(2,1)S(1)} %fusion.57) | copy-start | bytes 1572868
  80.9 62.5 %copy-start.15 = (bf16[4,1024,512]{2,1,0:T(8,128)(2,1)S(1)}, bf16[4,1024,512]{2,1,0:T(8,128)(2,1)}, u32[]{:S(2)}) copy-start(bf16[4,1024,512]{2,1,0:T(8,128)(2,1)} %param.26) | copy-start | bytes 12582916
  143.4 4.1 copy-start.14
  147.4 5.6 copy-start.45
  147.4 5.6 copy-start.44
  161.2 5.3 copy-start.38
  161.2 5.5 copy-start.39
  161.2 5.7 copy-start.26
  161.2 64.7 %all-to-all-start.1 = ((bf16[4,4,160,1024]{3,2,1,0:T(8,128)(2,1)}), bf16[4,4,160,1024]{3,2,1,0:T(8,128)(2,1)}, u32[]{:S(2)}, u32[]{:S(2)}) async-start(bf16[4,4,160,1024]{3,2,1,0:T(8,128)(2,1)} %copy.89), calls=%async_computation.1 | async-start | bytes 10485760 | tf_op jit(solution)/shard_map/all_to_all | solution.py:183
  342.0 8.6 copy-start.16
  362.5 64.5 %all-to-all-start.3 = ((bf16[4,4,160,1024]{3,2,1,0:T(8,128)(2,1)}), bf16[4,4,160,1024]{3,2,1,0:T(8,128)(2,1)}, u32[]{:S(2)}, u32[]{:S(2)}) async-start(bf16[4,4,160,1024]{3,2,1,0:T(8,128)(2,1)} %copy.92), calls=%async_computation.3 | async-start | bytes 10485760 | tf_op jit(solution)/shard_map/all_to_all | solution.py:220
  367.6 140.2 %reduce-scatter.3.cloned.1.call-start = ((), (), s32[]{:S(2)}) async-start(), calls=%async_computation.6 | async-start | bytes 1572864 | tf_op jit(solution)/shard_map/reduce_scatter | solution.py:277
  441.2 8.1 copy-start.5
  441.2 8.6 copy-start.27
  449.8 5.8 copy-start.23
  455.5 5.3 slice-start
  455.5 6.1 slice-start.1
  461.6 4.4 copy-start.19
  461.6 4.4 copy-start.21
  468.4 44.2 %reduce-scatter.5.cloned.1.call-start = ((), (), s32[]{:S(2)}) async-start(), calls=%async_computation.7 | async-start | bytes 1572864 | tf_op jit(solution)/shard_map/reduce_scatter | solution.py:280
  474.7 420.3 %all-reduce.8.cloned.1.call-start = ((), (), s32[]{:S(2)}) async-start(), calls=%async_computation.9 | async-start | bytes 25165824 | tf_op jit(solution)/shard_map/psum | solution.py:309
  475.0 8.9 copy-start.17
  475.0 17.4 %slice-start.2 = ((s8[5242880]{0:T(1024)(128)(4,1)}), s8[4194304]{0:T(1024)(128)(4,1)S(1)}, s32[]{:S(2)}) async-start(s8[5242880]{0:T(1024)(128)(4,1)} %bitcast.293), calls=%async_computation.12 | async-start | bytes 8388608
  483.9 8.4 slice-start.3
  483.9 8.4 copy-start.46
  497.5 4.2 copy-start.33
  497.5 4.2 copy-start.35
  497.5 641.1 %all-reduce.6.cloned.1.call-start = ((), (), s32[]{:S(2)}) async-start(), calls=%async_computation.8 | async-start | bytes 25296896 | tf_op jit(solution)/shard_map/psum | solution.py:313
  498.6 3.3 copy-start.37
  498.6 3.3 copy-start.42
  501.7 3.4 copy-start.7
  501.7 3.4 copy-start.29
  515.6 4.2 copy-start.30
  515.6 4.2 copy-start.31
  895.1 6.9 copy-start.12
  902.0 4.6 copy-start.11
  1138.7 4.9 copy-start.25
  1138.7 6.3 copy-start.24
  1143.6 3.7 copy-start.13
  (9 other events, 17.3 us)
Sparse Core Ops, SparseCore 0:
  468.6 20.5 reduce-scatter.2
  492.1 20.4 reduce-scatter.4
Sparse Core Ops, SparseCore 1:
  497.6 397.4 all-reduce.7
  903.6 235.0 all-reduce.5
where the time goes:
time: 1170 us; the launch traced here: 1160 us
  waiting for transfers between devices  675 us (58%)
  blocking collectives  187 us (16%)
  matrix products  114 us (10%)
  local copies, waits for them, and re-layouts  94.5 us (8%)
  other arithmetic  60.2 us (5%)
  between operations  16.8 us (1%)
    psum x1, waiting for transfers between devices, body(): lax.psum(grad_gate_w.astype(jnp.bfloat16), ('context', 'dp'))  328 us
    psum x1, waiting for transfers between devices, body(): lax.psum((grad_gain_one, grad_query_w, grad_key_w, grad_value_w, grad_out...  228 us
    all_to_all x1, blocking collectives, body(): lax.all_to_all(grad_slots, 'expert', split_axis=0, concat_axis=0, tiled=T...  63.3 us
    all_to_all x1, blocking collectives, body(): lax.all_to_all(sent_rows, 'expert', split_axis=0, concat_axis=0, tiled=True)  62.5 us
    all_to_all x1, waiting for transfers between devices, body(): lax.all_to_all(grad_sent, 'expert', split_axis=0, concat_axis=0, tiled=True)  59.2 us
    all_to_all x1, waiting for transfers between devices, body(): lax.all_to_all(produced, 'expert', split_axis=0, concat_axis=0, tiled=True)  57.9 us
    psum x1, blocking collectives, body(): lax.psum((grad_gain_one, grad_query_w, grad_key_w, grad_value_w, grad_out...  42.8 us
    unnamed x110, local copies, waits for them, and re-layouts  23.9 us
  transfers between devices with their start and end apart: 6, of which 5 were waited for; matrix products, arithmetic and copies ran while one was open for 6% of the time, Pallas kernels for 0%

commit v1 on v0

--- a/solution.py
+++ b/solution.py
@@ -311,16 +311,19 @@
         lax.psum(grad_down_w.astype(jnp.bfloat16), ("context", "dp")).astype(jnp.float32),
     )
     total_g1, total_q, total_k, total_v, total_o, total_g2, total_r = lax.psum(
-        (
-            grad_gain_one,
-            grad_query_w,
-            grad_key_w,
-            grad_value_w,
-            grad_out_w,
-            grad_gain_two,
-            grad_router_w,
+        lax.psum(
+            (
+                grad_gain_one,
+                grad_query_w,
+                grad_key_w,
+                grad_value_w,
+                grad_out_w,
+                grad_gain_two,
+                grad_router_w,
+            ),
+            ("context", "dp"),
         ),
-        ("expert", "context", "dp"),
+        "expert",
     )
     return (
         outputs,

time: 1170 us -> 1580 us (1.35)
  waiting for transfers between devices: 675 us -> 1100 us
  blocking collectives: 187 us -> 171 us
    psum x0 -> x1, waiting for transfers between devices: none -> 209 us  [body(): lax.psum(lax.psum((grad_gain_one, grad_query_w, grad_key_w, grad_value_w,...]
    psum x1, waiting for transfers between devices: 228 us -> 383 us  [body(): lax.psum((grad_gain_one, grad_query_w, grad_key_w, grad_value_w, grad_out...]
    psum x1, waiting for transfers between devices: 328 us -> 369 us  [body(): lax.psum(grad_gate_w.astype(jnp.bfloat16), ('context', 'dp'))]
    psum x1, blocking collectives: 42.8 us -> 20.5 us  [body(): lax.psum((grad_gain_one, grad_query_w, grad_key_w, grad_value_w, grad_out...]
    reduce_scatter x1, waiting for transfers between devices: 1.83 us -> 20.2 us  [body(): lax.psum_scatter(grad_values.reshape(seq_rows, KV * HD), 'context', scatt...]
  transfers between devices with their start and end apart: 6 -> 7, of which waited for: 5 -> 7; matrix products, arithmetic and copies ran while one was open for 6% -> 4% of each run, Pallas kernels for 0% -> 0%
where the time goes in v1:
time: 1580 us; the launch traced here: 1570 us
  waiting for transfers between devices  1100 us (70%)
  blocking collectives  171 us (11%)
  matrix products  114 us (7%)
  local copies, waits for them, and re-layouts  94.6 us (6%)
  other arithmetic  60.3 us (4%)
    psum x1, waiting for transfers between devices, body(): lax.psum((grad_gain_one, grad_query_w, grad_key_w, grad_value_w, grad_out...  383 us
    psum x1, waiting for transfers between devices, body(): lax.psum(grad_gate_w.astype(jnp.bfloat16), ('context', 'dp'))  369 us
    psum x1, waiting for transfers between devices, body(): lax.psum(lax.psum((grad_gain_one, grad_query_w, grad_key_w, grad_value_w,...  209 us
    all_to_all x1, blocking collectives, body(): lax.all_to_all(grad_slots, 'expert', split_axis=0, concat_axis=0, tiled=T...  63.3 us
    all_to_all x1, blocking collectives, body(): lax.all_to_all(sent_rows, 'expert', split_axis=0, concat_axis=0, tiled=True)  62.5 us
    all_to_all x1, waiting for transfers between devices, body(): lax.all_to_all(grad_sent, 'expert', split_axis=0, concat_axis=0, tiled=True)  59.2 us
    all_to_all x1, waiting for transfers between devices, body(): lax.all_to_all(produced, 'expert', split_axis=0, concat_axis=0, tiled=True)  57.9 us
  transfers between devices with their start and end apart: 7, of which 7 were waited for; matrix products, arithmetic and copies ran while one was open for 4% of the time, Pallas kernels for 0%

profile of v1, /device:TPU:0, one launch (start us, length us, event | category | flops | bytes accessed | tf_op | source)
XLA Modules:
  0.0 1569.1 jit_solution(11471794016647284078)
XLA Ops:
  13.0 9.9 all_gather.8
  29.8 8.2 all_gather.9
  38.0 4.1 copy.81
  52.5 4.5 reduce-window.6
  57.9 8.1 scatter_custom_fusion
  67.6 8.8 gather_fusion
  76.4 3.7 select_select_fusion
  80.1 62.5 %all_to_all.20 = bf16[4,4,160,1024]{3,2,1,0:T(8,128)(2,1)S(1)} all-to-all(bf16[4,4,160,1024]{3,2,1,0:T(8,128)(2,1)S(1)} %select_select_fusion), channel_id=1, replica_groups=mesh['expert'=4,'context'=2,'dp'=4] {'expert'}, dimensions={0} | all-to-all | bytes 10485760 | tf_op jit(solution)/shard_map/all_to_all | solution.py:174
  142.6 2.9 fusion.26
  146.6 5.4 fusion.15
  152.3 4.9 convert_bitcast_fusion.1
  157.1 3.3 copy.89
  160.4 5.2 all-to-all-start.1
  167.2 57.9 %all-to-all-done.1 = bf16[4,4,160,1024]{3,2,1,0:T(8,128)(2,1)} async-done(((bf16[4,4,160,1024]{3,2,1,0:T(8,128)(2,1)}), bf16[4,4,160,1024]{3,2,1,0:T(8,128)(2,1)}, u32[]{:S(2)}, u32[]{:S(2)}) %all-to-all-start.1) | async-done | bytes 5242912 | tf_op jit(solution)/shard_map/all_to_all | solution.py:183
  225.1 14.1 gather_fusion.2
  239.2 3.3 fusion.2
  242.9 3.4 bitcast_multiply_fusion.1
  246.3 14.8 gather_fusion.1
  261.1 4.0 select_convert_fusion
  265.1 63.3 %all_to_all.21 = bf16[4,4,160,1024]{3,2,1,0:T(8,128)(2,1)} all-to-all(bf16[4,4,160,1024]{3,2,1,0:T(8,128)(2,1)S(1)} %select_convert_fusion), channel_id=1, replica_groups=mesh['expert'=4,'context'=2,'dp'=4] {'expert'}, dimensions={0} | all-to-all | bytes 10485760 | tf_op jit(solution)/shard_map/all_to_all | solution.py:196
  328.4 12.7 fusion.13
  341.2 8.6 fusion.29
  349.8 8.9 fusion.10
  358.8 3.0 copy.92
  361.8 5.1 all-to-all-start.3
  367.1 59.2 %all-to-all-done.3 = bf16[4,4,160,1024]{3,2,1,0:T(8,128)(2,1)} async-done(((bf16[4,4,160,1024]{3,2,1,0:T(8,128)(2,1)}), bf16[4,4,160,1024]{3,2,1,0:T(8,128)(2,1)}, u32[]{:S(2)}, u32[]{:S(2)}) %all-to-all-start.3) | async-done | bytes 5242912 | tf_op jit(solution)/shard_map/all_to_all | solution.py:220
  426.3 14.1 gather_fusion.3
  440.4 8.1 convert_reduce_fusion
  454.8 5.3 fusion.3
  468.6 6.3 fusion.38
  475.2 3.0 convolution_multiply_fusion
  478.5 2.9 fusion.76
  481.3 2.7 fusion.79
  484.1 4.4 reduce-scatter.3.cloned.1.call-done
  491.5 20.2 %reduce-scatter.5.cloned.1.call-done = f32[256,512]{0,1:T(8,128)} async-done(((f32[512,512]{0,1:T(8,128)}), f32[256,512]{0,1:T(8,128)}) %reduce-scatter.5.cloned.1.call-update) | async-done | bytes 524304 | tf_op jit(solution)/shard_map/reduce_scatter | solution.py:280
  511.7 2.9 fusion.82
  514.7 8.9 bitcast_convert_fusion.2
  523.6 8.7 bitcast_convert_fusion.1
  532.4 5.1 bitcast_convert_fusion
  537.8 382.9 %all-reduce.9.cloned.1.call-done = (f32[1024,1024]{1,0:T(8,128)}, f32[1024,512]{1,0:T(8,128)}, f32[1024,512]{1,0:T(8,128)}, f32[1024,1024]{1,0:T(8,128)}, f32[1024,16]{0,1:T(8,128)}) async-done(((f32[1024,1024]{1,0:T(8,128)}, f32[1024,512]{1,0:T(8,128)}, f32[1024,512]{1,0:T(8,128)}, f32[1024,1024]{1,0:T(8,128)}, f32[1024,16]{0,1:T(8,128)}), (f32[1024,1024]{1,0:T(8,128)}, f32[1024,512]{1,0:T(8,128)}, ...) | async-done | bytes 12648464 | tf_op jit(solution)/shard_map/psum | solution.py:314
  926.6 20.5 %all-reduce = (f32[1024]{0:T(1024)S(1)}, f32[1024]{0:T(1024)S(1)}) all-reduce(f32[1024]{0:T(1024)S(1)} %get-tuple-element.15, f32[1024]{0:T(1024)S(1)} %get-tuple-element.13), channel_id=1, replica_groups=mesh['expert'=4,'context'=2,'dp'=4] {'context','dp'}, use_global_device_ids=true, to_apply=%region_24.26 | all-reduce | flops 2048 | bytes 16384 | tf_op jit(solution)/shard_map/psum | solution.py:314
  947.1 6.7 all-reduce.2
  956.5 369.3 %all-reduce.13.cloned.1.call-done = (bf16[4,1024,512]{2,1,0:T(8,128)(2,1)}, bf16[4,1024,512]{2,1,0:T(8,128)(2,1)}, bf16[4,512,1024]{2,1,0:T(8,128)(2,1)}) async-done(((bf16[4,1024,512]{2,1,0:T(8,128)(2,1)}, bf16[4,1024,512]{2,1,0:T(8,128)(2,1)}, bf16[4,512,1024]{2,1,0:T(8,128)(2,1)}), (bf16[4,1024,512]{2,1,0:T(8,128)(2,1)}, bf16[4,1024,512]{2,1,0:T(8,128)(2,1)}, ...) | async-done | bytes 12582928 | tf_op jit(solution)/shard_map/psum | solution.py:309
  1325.8 6.9 convert_element_type.232
  1332.7 4.6 convert_element_type.234
  1337.3 4.4 convert_element_type.236
  1341.8 209.0 %all-reduce.11.cloned.1.call-done = (f32[1024,1024]{1,0:T(8,128)}, f32[1024,512]{1,0:T(8,128)}, f32[1024,512]{1,0:T(8,128)}, f32[1024,1024]{1,0:T(8,128)}, f32[1024,16]{0,1:T(8,128)}) async-done(((f32[1024,1024]{1,0:T(8,128)}, f32[1024,512]{1,0:T(8,128)}, f32[1024,512]{1,0:T(8,128)}, f32[1024,1024]{1,0:T(8,128)}, f32[1024,16]{0,1:T(8,128)}), (f32[1024,1024]{1,0:T(8,128)}, f32[1024,512]{1,0:T(8,128)}, ...) | async-done | bytes 12648464 | tf_op jit(solution)/shard_map/psum | solution.py:313
  1550.8 4.9 copy.147
  (198 shorter events, 62.4 us)
Async XLA Ops:
  7.2 43.3 %copy-start = (bf16[1024,1024]{1,0:T(8,128)(2,1)S(1)}, bf16[1024,1024]{1,0:T(8,128)(2,1)}, u32[]{:S(2)}) copy-start(bf16[1024,1024]{1,0:T(8,128)(2,1)} %param.23) | copy-start | bytes 6291460
  7.2 20.5 %copy-start.3 = (bf16[1,256,1024]{2,1,0:T(8,128)(2,1)S(1)}, bf16[1,256,1024]{2,1,0:T(8,128)(2,1)}, u32[]{:S(2)}) copy-start(bf16[1,256,1024]{2,1,0:T(8,128)(2,1)} %param.16) | copy-start | bytes 1572868
  9.8 32.3 %copy-start.36 = (f32[1024]{0:T(1024)}, f32[1024]{0:T(1024)S(1)}, u32[]{:S(2)}) copy-start(f32[1024]{0:T(1024)S(1)} %convert_element_type.188) | copy-start | bytes 12292
  11.1 31.0 %copy-start.41 = (f32[256]{0:T(256)}, f32[256]{0:T(256)S(1)}, u32[]{:S(2)}) copy-start(f32[256]{0:T(256)S(1)} %add_rsqrt_fusion.1) | copy-start | bytes 3076
  29.7 15.0 copy-start.32
  29.7 15.0 copy-start.34
  38.0 8.3 copy-start.8
  46.3 4.2 copy-start.1
  48.1 4.2 copy-start.43
  50.5 25.9 %copy-start.28 = (bf16[8,64,2,256]{3,1,2,0:T(8,128)(2,1)}, bf16[8,64,2,256]{3,1,2,0:T(8,128)(2,1)S(1)}, u32[]{:S(2)}) copy-start(bf16[8,64,2,256]{3,1,2,0:T(8,128)(2,1)S(1)} %fusion.57) | copy-start | bytes 1572868
  80.1 62.5 %copy-start.15 = (bf16[4,1024,512]{2,1,0:T(8,128)(2,1)S(1)}, bf16[4,1024,512]{2,1,0:T(8,128)(2,1)}, u32[]{:S(2)}) copy-start(bf16[4,1024,512]{2,1,0:T(8,128)(2,1)} %param.26) | copy-start | bytes 12582916
  142.6 4.1 copy-start.14
  146.6 5.6 copy-start.45
  146.6 5.6 copy-start.44
  160.4 5.3 copy-start.38
  160.4 5.5 copy-start.39
  160.4 5.7 copy-start.26
  160.4 64.7 %all-to-all-start.1 = ((bf16[4,4,160,1024]{3,2,1,0:T(8,128)(2,1)}), bf16[4,4,160,1024]{3,2,1,0:T(8,128)(2,1)}, u32[]{:S(2)}, u32[]{:S(2)}) async-start(bf16[4,4,160,1024]{3,2,1,0:T(8,128)(2,1)} %copy.89), calls=%async_computation.1 | async-start | bytes 10485760 | tf_op jit(solution)/shard_map/all_to_all | solution.py:183
  341.2 8.6 copy-start.16
  361.8 64.5 %all-to-all-start.3 = ((bf16[4,4,160,1024]{3,2,1,0:T(8,128)(2,1)}), bf16[4,4,160,1024]{3,2,1,0:T(8,128)(2,1)}, u32[]{:S(2)}, u32[]{:S(2)}) async-start(bf16[4,4,160,1024]{3,2,1,0:T(8,128)(2,1)} %copy.92), calls=%async_computation.3 | async-start | bytes 10485760 | tf_op jit(solution)/shard_map/all_to_all | solution.py:220
  366.8 121.6 %reduce-scatter.3.cloned.1.call-start = ((), (), s32[]{:S(2)}) async-start(), calls=%async_computation.6 | async-start | bytes 1572864 | tf_op jit(solution)/shard_map/reduce_scatter | solution.py:277
  440.4 8.1 copy-start.7
  440.4 8.6 copy-start.27
  449.0 5.8 copy-start.23
  454.8 5.3 slice-start
  454.8 6.1 slice-start.1
  460.9 4.5 copy-start.19
  460.9 4.5 copy-start.21
  467.7 44.0 %reduce-scatter.5.cloned.1.call-start = ((), (), s32[]{:S(2)}) async-start(), calls=%async_computation.7 | async-start | bytes 1572864 | tf_op jit(solution)/shard_map/reduce_scatter | solution.py:280
  468.6 6.6 copy-start.9
  474.9 3.3 copy-start.33
  474.9 3.5 copy-start.4
  474.9 3.5 copy-start.37
  474.9 3.5 copy-start.42
  474.9 445.8 %all-reduce.9.cloned.1.call-start = ((), (), s32[]{:S(2)}) async-start(), calls=%async_computation.8 | async-start | bytes 25296896 | tf_op jit(solution)/shard_map/psum | solution.py:314
  514.6 811.2 %all-reduce.13.cloned.1.call-start = ((), (), s32[]{:S(2)}) async-start(), calls=%async_computation.10 | async-start | bytes 25165824 | tf_op jit(solution)/shard_map/psum | solution.py:309
  514.7 8.9 copy-start.17
  514.7 17.7 %slice-start.2 = ((s8[5242880]{0:T(1024)(128)(4,1)}), s8[4194304]{0:T(1024)(128)(4,1)S(1)}, s32[]{:S(2)}) async-start(s8[5242880]{0:T(1024)(128)(4,1)} %bitcast.293), calls=%async_computation.13 | async-start | bytes 8388608
  523.6 8.7 slice-start.3
  523.6 8.7 copy-start.46
  537.5 1013.3 %all-reduce.11.cloned.1.call-start = ((), (), s32[]{:S(2)}) async-start(), calls=%async_computation.9 | async-start | bytes 25296896 | tf_op jit(solution)/shard_map/psum | solution.py:313
  920.7 4.2 copy-start.30
  920.7 4.2 copy-start.31
  1325.8 6.9 copy-start.12
  1332.7 4.6 copy-start.11
  1550.8 4.9 copy-start.25
  1550.8 6.3 copy-start.24
  1555.7 3.7 copy-start.13
  (10 other events, 22.5 us)
Sparse Core Ops, SparseCore 0:
  467.8 20.5 reduce-scatter.2
  491.3 20.3 reduce-scatter.4
  518.0 402.7 all-reduce.8
  926.5 399.2 all-reduce.12
  1328.6 222.1 all-reduce.10
